TPU v7x, 32 devices: a whole 2x2x4 slice. The times are simulated.
32 devices in a mesh: dom: 8 (over y, x, core), band: 4 (over z).
Axes of the slice: x: 2, y: 2, z: 4, core: 2. Of those that a mesh axis runs over, the one named last changes fastest.
Arguments:
- waves: float32 [2048, 2048], P('dom', 'band'), may hold values from -6 to 6
- cell_matrix: float32 [64, 125, 125], P('dom')
- connect: int32 [64, 125], P('dom'), may hold values from 0 to 383, as said below
- send_index: int32 [8, 2, 64], P('dom'), may hold values from 0 to 255
- rotation: float32 [2048, 2048], P('band'), may hold values from -0.125 to 0.125
Outputs:
- rotated: float32 [2048, 2048], P('dom', 'band')
Inputs may be any that keep to these rules, and one draw needn't show every extreme that they name: On domain d, an entry of connect at or above 256 is 256 + k * 64 + s where s is below the number of slots that domain (d - 1 + 2 k) mod 8 fills on face k: exactly 64 for k = 1, between 64 // 2 (at least 1) and 64, uneven over domains, for k = 0; only those slots of send_index matter.
All inputs are finite; a program needn't handle non-finite values.
Results may differ from a plain program's by a relative error of at most 0.00012.
Values sent between devices are 32-bit elements; how exact they have to be, the bound alone decides.
A program may use at most 64 MiB of HBM per device.

v0:
```python
import functools

import jax
import jax.numpy as jnp
from jax import lax
from jax.experimental import pallas as pl
from jax.experimental.pallas import tpu as pltpu
from jax.sharding import PartitionSpec as P

DEGREE = 8
LANES = 128


centre = 5.5
half_width = 9.5


def split(x):
    high = lax.reduce_precision(x, 8, 7)
    return high.astype(jnp.bfloat16), (x - high).astype(jnp.bfloat16)


def doubled(x, half):
    return x + pltpu.roll(x, half, 1)


def packed(x, half):
    high = x.astype(jnp.bfloat16)
    low = (x - high.astype(jnp.float32)).astype(jnp.bfloat16)
    lane = lax.broadcasted_iota(jnp.int32, x.shape, 1)
    return jnp.where(lane < half, high.astype(jnp.float32), low.astype(jnp.float32)).astype(
        jnp.bfloat16
    )


def mm(a, b):
    return jnp.dot(a, b, preferred_element_type=jnp.float32)


def filter_kernel(doms, owned, slots, half, high, low, pick, spread, start, out, pieces, ghosts, before, image):
    unroll = doms <= 8

    def over(body):
        if unroll:
            for d in range(doms):
                body(d)
        else:
            pl.loop(0, doms)(body)

    def begin(d):
        v = start[d]
        out[d] = v
        before[d] = jnp.zeros_like(v)
        pieces[d, :owned] = packed(v, half)

    over(begin)

    def one(step, _):
        def send(d):
            after = lax.rem(d + 1, doms) if not unroll else (d + 1) % doms
            ahead = lax.rem(d + doms - 1, doms) if not unroll else (d - 1) % doms
            g = mm(pick[d], pieces[d, :owned]).astype(jnp.bfloat16)
            pieces[after, owned : owned + slots] = g[:slots]
            pieces[ahead, owned + slots :] = g[slots:]

        over(send)

        def apply(d):
            x = pieces[d]
            y = mm(high[d], x) + mm(low[d], x)
            y = doubled(y, half)
            image[d] = y[:owned]
            after = lax.rem(d + 1, doms) if not unroll else (d + 1) % doms
            ahead = lax.rem(d + doms - 1, doms) if not unroll else (d - 1) % doms
            r = packed(y[owned:], half)
            ghosts[ahead, :slots] = r[:slots]
            ghosts[after, slots:] = r[slots:]

        over(apply)
        scale = jnp.where(step == 0, 1.0, 2.0)

        def update(d):
            y = image[d] + doubled(mm(spread[d], ghosts[d]), half)
            v = scale * y - before[d]
            before[d] = out[d]
            out[d] = v
            pieces[d, :owned] = packed(v, half)

        over(update)
        return 0

    lax.fori_loop(0, DEGREE, one, 0)


def shards(waves, cell_matrix, connect, send_index, rotation):
    owned = waves.shape[0]
    width = waves.shape[1]
    slots = send_index.shape[2]
    doms = lax.axis_size("dom")
    size = owned + 2 * slots
    seat = jax.nn.one_hot(connect, size, dtype=jnp.float32)
    half_way = jnp.einsum("cij,cjn->cin", cell_matrix, seat, precision=lax.Precision.HIGH)
    local = jnp.einsum("cim,cin->mn", seat, half_way, precision=lax.Precision.HIGH)
    node = jnp.arange(size)
    shift = jnp.where((node[:, None] == node[None, :]) & (node[:, None] < owned), centre, 0.0)
    local = (local - shift) / half_width
    row = jnp.zeros((8, size), jnp.float32).at[0, : 2 * slots].set(
        send_index.reshape(-1).astype(jnp.float32)
    )
    everyone = lax.all_gather(jnp.concatenate([local, row], axis=0), "dom")
    high, low = split(everyone[:, :size])
    index = everyone[:, size, : 2 * slots].astype(jnp.int32)
    pick = jax.nn.one_hot(index, owned, dtype=jnp.bfloat16)
    spread = jnp.swapaxes(pick, 1, 2)

    partial = jnp.dot(waves, rotation, precision=lax.Precision.HIGH, preferred_element_type=jnp.float32)
    turned = lax.psum_scatter(partial, "band", scatter_dimension=1, tiled=True)
    share = width // doms
    columns = lax.all_to_all(turned, "dom", split_axis=1, concat_axis=0, tiled=True)
    columns = columns.reshape(doms, owned, share)
    half = LANES // 2
    columns = jnp.pad(columns, ((0, 0), (0, 0), (0, half - share)))
    columns = jnp.concatenate([columns, columns], axis=2)
    vmem = pl.BlockSpec(memory_space=pltpu.VMEM)
    done = pl.pallas_call(
        functools.partial(filter_kernel, doms, owned, slots, half),
        out_shape=jax.ShapeDtypeStruct((doms, owned, LANES), jnp.float32),
        in_specs=[vmem] * 5,
        out_specs=vmem,
        scratch_shapes=[
            pltpu.VMEM((doms, size, LANES), jnp.bfloat16),
            pltpu.VMEM((doms, 2 * slots, LANES), jnp.bfloat16),
            pltpu.VMEM((doms, owned, LANES), jnp.float32),
            pltpu.VMEM((doms, owned, LANES), jnp.float32),
        ],
        compiler_params=pltpu.CompilerParams(vmem_limit_bytes=56 * 2**20),
        cost_estimate=pl.CostEstimate(
            flops=DEGREE * doms * 4 * size * size * LANES, bytes_accessed=2**24, transcendentals=0
        ),
    )(high, low, pick, spread, columns)
    back = done[:, :, :share].reshape(doms * owned, share)
    return lax.all_to_all(back, "dom", split_axis=0, concat_axis=1, tiled=True)


def solution(mesh):
    in_specs = (
        P("dom", "band"),
        P("dom", None, None),
        P("dom", None),
        P("dom", None, None),
        P("band", None),
    )
    out_specs = P("dom", "band")
    return jax.shard_map(shards, mesh=mesh, in_specs=in_specs, out_specs=out_specs, check_vma=False)
```

profile of v0, /device:TPU:0, one launch (start us, length us, event | category | flops | bytes accessed | tf_op | source)
XLA Modules:
  0.0 128.6 jit_solution(12877771795569388582)
XLA Ops:
  7.4 0.0 reduce-scatter.2.cloned.1.call-start
  7.4 1.0 copy-done
  8.4 5.5 %fusion.19 = f32[256,2048]{1,0:T(8,128)} fusion(f32[256,512]{1,0:T(8,128)S(1)} %copy-done, f32[512,2048]{1,0:T(8,128)} %param.11), kind=kOutput, calls=%fused_computation.24 | convolution fusion | flops 1610612736 | bytes 6815744 | tf_op jit(solution)/shard_map/dot_general | solution.py:116
  14.0 0.0 reduce-scatter.2.cloned.1.call-update
  14.0 0.0 all-gather.3.cloned.1.call-start
  14.1 0.1 convert_element_type.36
  14.1 0.8 copy-done.1
  15.0 0.7 fusion.3
  15.7 1.1 fusion.10
  16.8 0.8 select_maximum_fusion
  17.6 0.0 all-gather.3.cloned.1.call-update
  17.7 43.0 %reduce-scatter.2.cloned.1.call-done = f32[256,512]{1,0:T(8,128)} async-done(((f32[256,2048]{1,0:T(8,128)}), f32[256,512]{1,0:T(8,128)}) %reduce-scatter.2.cloned.1.call-update) | async-done | bytes 524304 | tf_op jit(solution)/shard_map/reduce_scatter | solution.py:117
  60.7 1.2 copy.12
  61.9 13.2 %all_to_all.32 = f32[256,8,64]{0,2,1:T(8,128)S(1)} all-to-all(f32[256,8,64]{0,2,1:T(8,128)S(1)} %bitcast.28), channel_id=1, replica_groups=mesh['dom'=8,'band'=4] {'dom'}, dimensions={1} | all-to-all | bytes 1048576 | tf_op jit(solution)/shard_map/all_to_all | solution.py:119
  75.1 0.3 copy.13
  75.5 1.3 %pad_maximum_fusion.start = f32[8,256,128]{2,1,0:T(8,128)} fusion(f32[8,256,64]{2,1,0:T(8,128)S(1)} %bitcast.27), kind=kLoop, calls=%fused_computation.10 | loop fusion | flops 262144 | bytes 1572864 | tf_op jit(solution)/shard_map/concatenate | solution.py:123
  76.8 5.5 %fusion = (bf16[8,384,384]{2,1,0:T(8,128)(2,1)}, bf16[8,384,384]{2,1,0:T(8,128)(2,1)}) fusion(f32[8,392,384]{2,1,0:T(8,128)} %bitcast.25), kind=kLoop, calls=%fused_computation.2 | loop fusion | flops 4718592 | bytes 9437184 | tf_op jit(solution)/shard_map/convert_element_type | solution.py:20
  82.3 0.8 slice_convert_fusion
  83.1 1.0 fusion.13.pick
  84.1 0.9 fusion.14.spread
  85.0 21.5 %shard_map.55 = f32[8,256,128]{2,1,0:T(8,128)} custom-call(bf16[8,384,384]{2,1,0:T(8,128)(2,1)} %get-tuple-element.18.high, bf16[8,384,384]{2,1,0:T(8,128)(2,1)} %get-tuple-element.17.low, bf16[8,128,256]{2,1,0:T(8,128)(2,1)} %fusion.13.pick, bf16[8,256,128]{2,1,0:T(8,128)(2,1)} %fusion.14.spread, f32[8,256,128]{2,1,0:T(8,128)} %pad_maximum_fusion.start), custom_call_target="tpu_custom_call" | custom-call | flops 4831838208 | bytes 16777216 | tf_op jit(solution)/shard_map/pallas_call | solution.py:125
  106.5 1.5 %copy.14 = f32[8,256,64]{1,2,0:T(8,128)S(1)} copy(f32[8,256,64]{2,1,0:T(8,128)} %bitcast.30) | data formatting | bytes 1048576 | tf_op jit(solution)/shard_map/slice | solution.py:141
  108.0 12.2 %all_to_all.33 = f32[8,256,64]{1,2,0:T(8,128)S(1)} all-to-all(f32[8,256,64]{1,2,0:T(8,128)S(1)} %copy.14), channel_id=1, replica_groups=mesh['dom'=8,'band'=4] {'dom'}, dimensions={0} | all-to-all | bytes 1048576 | tf_op jit(solution)/shard_map/all_to_all | solution.py:142
  120.2 1.0 copy.15
  (9 shorter events, 0.0 us)
Async XLA Ops:
  7.4 1.0 copy-start
  7.4 6.7 %copy-start.3 = (s32[1,2,64]{2,1,0:T(2,128)S(1)}, s32[1,2,64]{2,1,0:T(2,128)}, u32[]{:S(2)}) copy-start(s32[1,2,64]{2,1,0:T(2,128)} %param.10) | copy-start | bytes 1540
  7.4 6.8 %copy-start.2 = (s32[8,125]{1,0:T(8,128)S(1)}, s32[8,125]{1,0:T(8,128)}, u32[]{:S(2)}) copy-start(s32[8,125]{1,0:T(8,128)} %param.9) | copy-start | bytes 12004
  7.4 53.3 %reduce-scatter.2.cloned.1.call-start = ((), (), s32[]{:S(2)}) async-start(), calls=%async_computation.3 | async-start | bytes 2621440 | tf_op jit(solution)/shard_map/reduce_scatter | solution.py:117
  14.0 1.0 copy-start.1
  14.0 62.8 %all-gather.3.cloned.1.call-start = ((), (), s32[]{:S(2)}) async-start(), calls=%async_computation.4 | async-start | bytes 5419008 | tf_op jit(solution)/shard_map/all_gather | solution.py:110
Sparse Core Ops, SparseCore 0:
  14.1 46.5 reduce-scatter.1
Sparse Core Ops, SparseCore 1:
  17.8 41.8 all-gather.2
where the time goes:
time: 129 us
  waiting for transfers between devices  43.1 us (33%)
  blocking collectives  25.3 us (20%)
  Pallas kernels  21.5 us (17%)
  between operations  14.9 us (12%)
  other arithmetic  10.4 us (8%)
  matrix products  7.34 us (6%)
  local copies, waits for them, and re-layouts  6.06 us (5%)
    reduce_scatter x1, waiting for transfers between devices, shards(): turned = lax.psum_scatter(partial, 'band', scatter_dimension=1, tiled=True)  43 us
    pallas_call x1, Pallas kernels, shards(): pl.pallas_call(functools.partial(filter_kernel, doms, owned, slots, half)...  21.5 us
    all_to_all x1, blocking collectives, shards(): lax.all_to_all(turned, 'dom', split_axis=1, concat_axis=0, tiled=True)  13.2 us
    all_to_all x1, blocking collectives, shards(): return lax.all_to_all(back, 'dom', split_axis=0, concat_axis=1, tiled=True)  12.2 us
    dot_general x1, matrix products, shards(): jnp.dot(waves, rotation, precision=lax.Precision.HIGH, preferred_element_...  5.54 us
    convert_element_type x1, other arithmetic, split(): return (high.astype(jnp.bfloat16), (x - high).astype(jnp.bfloat16))  5.52 us
  transfers between devices with their start and end apart: 2, of which 1 were waited for; matrix products, arithmetic and copies ran while one was open for 4% of the time, Pallas kernels for 0%

commit v1 on v0

--- a/solution.py
+++ b/solution.py
@@ -9,6 +9,7 @@
 
 DEGREE = 8
 LANES = 128
+MESH = pl.DeviceIdType.MESH
 
 
 centre = 5.5
@@ -92,11 +93,331 @@
     lax.fori_loop(0, DEGREE, one, 0)
 
 
+def high_low(x):
+    high = x.astype(jnp.bfloat16)
+    return high, (x - high.astype(jnp.float32)).astype(jnp.bfloat16)
+
+
+def fused_kernel(bands, owned, slots, waves, cells, conn, send, rotation, out, *scratch):
+    (acc, from_left, from_right, everyone, matrix, pick, spread, sendbuf, colrecv, pieces, ghosts,
+     state, before, image, sendback, backrecv,
+     z_send, z_right, z_left, m_send, m_recv, a_send, a_recv, b_send, b_recv) = scratch
+    doms = 8
+    width = waves.shape[1]
+    size = owned + 2 * slots
+    half = LANES // 2
+    rows = owned // 2
+    me = lax.axis_index("dom")
+    z = lax.axis_index("band")
+    core = lax.rem(me, 2)
+    place = lax.rem(lax.div(me, 2), 2)
+    upper = lax.div(me, 4)
+    sib = me + 1 - 2 * core
+    x_next = me + 2 - 4 * place
+    y_next = me + 4 - 8 * upper
+    diag = x_next + 4 - 8 * upper
+
+    barrier = pltpu.get_barrier_semaphore()
+    for t in range(1, doms):
+        pl.semaphore_signal(barrier, inc=1, device_id={"dom": lax.rem(me + t, doms)}, device_id_type=MESH)
+
+    @pl.when(z > 0)
+    def _():
+        pl.semaphore_signal(barrier, inc=1, device_id={"band": z - 1}, device_id_type=MESH)
+
+    @pl.when(z < bands - 1)
+    def _():
+        pl.semaphore_signal(barrier, inc=1, device_id={"band": z + 1}, device_id_type=MESH)
+
+    beside = lax.div(z + bands - 1, bands) + lax.div(2 * bands - 2 - z, bands)
+    pl.semaphore_wait(barrier, doms - 1 + beside)
+
+    def to_right(j):
+        return pltpu.make_async_remote_copy(
+            src_ref=acc.at[j], dst_ref=from_left.at[j], send_sem=z_send.at[j],
+            recv_sem=z_right.at[j], device_id={"band": z + 1}, device_id_type=MESH)
+
+    def to_left(j):
+        return pltpu.make_async_remote_copy(
+            src_ref=acc.at[j], dst_ref=from_right.at[j], send_sem=z_send.at[j],
+            recv_sem=z_left.at[j], device_id={"band": z - 1}, device_id_type=MESH)
+
+    order = []
+    for r in range(bands // 2):
+        order += [bands - 1 - r, r]
+    w_high, w_low = high_low(waves[...])
+    for j in order:
+        r_high, r_low = high_low(rotation[:, j * width : (j + 1) * width])
+        acc[j] = mm(w_high, r_high) + (mm(w_high, r_low) + mm(w_low, r_high))
+        if j > 0:
+            @pl.when(z == 0)
+            def _():
+                to_right(j).start()
+        if j < bands - 1:
+            @pl.when(z == bands - 1)
+            def _():
+                to_left(j).start()
+
+    node = lax.broadcasted_iota(jnp.int32, (size, conn.shape[1]), 0)
+    total = jnp.zeros((size, size), jnp.float32)
+    for c in range(cells.shape[0]):
+        seat = jnp.where(node == conn[c : c + 1, :], 1.0, 0.0).astype(jnp.bfloat16)
+        a_high, a_low = high_low(cells[c])
+        b_high, b_low = high_low(mm(seat, a_high) + mm(seat, a_low))
+        dims = (((1,), (1,)), ((), ()))
+        total = total + (
+            lax.dot_general(b_high, seat, dims, preferred_element_type=jnp.float32)
+            + lax.dot_general(b_low, seat, dims, preferred_element_type=jnp.float32))
+    r_at = lax.broadcasted_iota(jnp.int32, (size, size), 0)
+    c_at = lax.broadcasted_iota(jnp.int32, (size, size), 1)
+    shift = jnp.where((r_at == c_at) & (r_at < owned), centre, 0.0)
+    everyone[me, :size] = (total - shift) / half_width
+    everyone[me, size:] = jnp.zeros((8, size), jnp.float32)
+    everyone[me, size : size + 2, :slots] = send[0].astype(jnp.float32)
+
+    def pass_on(slot, to, k):
+        return pltpu.make_async_remote_copy(
+            src_ref=everyone.at[slot], dst_ref=everyone.at[slot], send_sem=m_send.at[k],
+            recv_sem=m_recv.at[slot], device_id={"dom": to}, device_id_type=MESH)
+
+    sent = [pass_on(me, x_next, 0), pass_on(me, y_next, 1), pass_on(me, sib, 2)]
+    for copy in sent:
+        copy.start()
+
+    def relay_right(j, at):
+        @pl.when(z == at)
+        def _():
+            to_right(j).wait_recv()
+            acc[j] = acc[j] + from_left[j]
+            to_right(j).start()
+
+    def relay_left(j, at):
+        @pl.when(z == at)
+        def _():
+            to_left(j).wait_recv()
+            acc[j] = acc[j] + from_right[j]
+            to_left(j).start()
+
+    pass_on(x_next, sib, 0).wait_recv()
+    pass_on(y_next, sib, 0).wait_recv()
+    relays = [
+        pass_on(x_next * (1 - core) + y_next * core, y_next * (1 - core) + x_next * core, 3),
+        pass_on(x_next, sib, 4),
+        pass_on(y_next, sib, 5),
+    ]
+    for copy in relays:
+        copy.start()
+    relay_right(3, 1)
+    relay_left(0, 2)
+    pass_on(diag, sib, 6).wait_recv()
+    last = pass_on(diag, sib, 6)
+    last.start()
+    relay_left(0, 1)
+    relay_right(3, 2)
+    relay_right(2, 1)
+    relay_left(1, 2)
+
+    lane = lax.broadcasted_iota(jnp.int32, (rows, LANES), 1)
+    low_lanes = lane < half
+
+    def prepare(d):
+        m_high, m_low = high_low(everyone[d, :size])
+        matrix[d, :, :size] = m_high
+        matrix[d, :, size:] = m_low
+        tile = everyone[d, size:, :LANES]
+        other = pltpu.roll(tile, half, 1)
+        first_lanes = lax.broadcasted_iota(jnp.int32, (1, LANES), 1) < half
+        row = jnp.where(first_lanes, tile[0:1], other[1:2]).astype(jnp.int32)
+        at = lax.broadcasted_iota(jnp.int32, (owned, LANES), 0)
+        hot = jnp.where(at == row, 1.0, 0.0)
+        spread[d] = hot.astype(jnp.bfloat16)
+        pick[d] = jnp.transpose(hot).astype(jnp.bfloat16)
+
+    sib_slots = [sib, x_next + 1 - 2 * core, y_next + 1 - 2 * core, diag + 1 - 2 * core]
+    for slot in sib_slots:
+        pass_on(slot, sib, 6).wait_recv()
+    for d in range(doms):
+        prepare(d)
+
+    finished = acc.at[z]
+    for j in range(bands):
+        if j > 0:
+            @pl.when(z == j)
+            def _():
+                to_right(j).wait_recv()
+                acc[j] = acc[j] + from_left[j]
+        if j < bands - 1:
+            @pl.when(z == j)
+            def _():
+                to_left(j).wait_recv()
+                acc[j] = acc[j] + from_right[j]
+
+    for p in range(doms // 2):
+        top = finished[:rows, p * LANES : (p + 1) * LANES]
+        bottom = finished[rows:, p * LANES : (p + 1) * LANES]
+        sendbuf[2 * p] = jnp.where(low_lanes, top, pltpu.roll(bottom, half, 1))
+        sendbuf[2 * p + 1] = jnp.where(low_lanes, pltpu.roll(top, half, 1), bottom)
+
+    def exchange(t):
+        to = lax.rem(me + t, doms)
+        return pltpu.make_async_remote_copy(
+            src_ref=sendbuf.at[to], dst_ref=colrecv.at[me], send_sem=a_send.at[t],
+            recv_sem=a_recv.at[me], device_id={"dom": to}, device_id_type=MESH)
+
+    def arrival(t):
+        frm = lax.rem(me + t, doms)
+        return pltpu.make_async_remote_copy(
+            src_ref=sendbuf.at[frm], dst_ref=colrecv.at[frm], send_sem=a_send.at[t],
+            recv_sem=a_recv.at[frm], device_id={"dom": frm}, device_id_type=MESH)
+
+    for t in range(1, doms):
+        exchange(t).start()
+    colrecv[me] = sendbuf[me]
+    for t in range(1, doms):
+        arrival(t).wait_recv()
+
+    def put(d, v):
+        x = packed(v, half)
+        pieces[d, :owned] = x
+        pieces[d, size : size + owned] = x
+
+    for d in range(doms):
+        blk = colrecv[d]
+        turned = pltpu.roll(blk, half, 1)
+        v = jnp.concatenate(
+            [jnp.where(low_lanes, blk, turned), jnp.where(low_lanes, turned, blk)], axis=0)
+        state[d] = v
+        before[d] = jnp.zeros_like(v)
+        put(d, v)
+
+    def spread_step():
+        for d in range(doms):
+            after, ahead = (d + 1) % doms, (d - 1) % doms
+            g = mm(pick[d], pieces[d, :owned]).astype(jnp.bfloat16)
+            for base in (0, size):
+                pieces[after, base + owned : base + owned + slots] = g[:slots]
+                pieces[ahead, base + owned + slots : base + size] = g[slots:]
+        for d in range(doms):
+            after, ahead = (d + 1) % doms, (d - 1) % doms
+            y = doubled(mm(matrix[d], pieces[d]), half)
+            image[d] = y[:owned]
+            r = packed(y[owned:], half)
+            ghosts[ahead, :slots] = r[:slots]
+            ghosts[after, slots:] = r[slots:]
+
+    def following(d, scale):
+        y = image[d] + doubled(mm(spread[d], ghosts[d]), half)
+        return scale * y - before[d]
+
+    def one(step, _):
+        spread_step()
+        scale = jnp.where(step == 0, 1.0, 2.0)
+        for d in range(doms):
+            v = following(d, scale)
+            before[d] = state[d]
+            state[d] = v
+            put(d, v)
+        return 0
+
+    lax.fori_loop(0, DEGREE - 1, one, 0)
+    spread_step()
+
+    def give(d):
+        return pltpu.make_async_remote_copy(
+            src_ref=sendback.at[d], dst_ref=backrecv.at[me], send_sem=b_send.at[d],
+            recv_sem=b_recv.at[me], device_id={"dom": d}, device_id_type=MESH)
+
+    for d in range(doms):
+        v = following(d, 2.0)
+        sendback[d] = jnp.where(low_lanes, v[:rows], v[rows:])
+
+        @pl.when(me != d)
+        def _():
+            give(d).start()
+
+    backrecv[me] = sendback[me]
+    for d in range(doms):
+        @pl.when(me != d)
+        def _():
+            pltpu.make_async_remote_copy(
+                src_ref=sendback.at[d], dst_ref=backrecv.at[d], send_sem=b_send.at[d],
+                recv_sem=b_recv.at[d], device_id={"dom": d}, device_id_type=MESH).wait_recv()
+
+    for p in range(doms // 2):
+        even, odd = backrecv[2 * p], backrecv[2 * p + 1]
+        columns = slice(p * LANES, (p + 1) * LANES)
+        out[:rows, columns] = jnp.where(low_lanes, even, pltpu.roll(odd, half, 1))
+        out[rows:, columns] = jnp.where(low_lanes, pltpu.roll(even, half, 1), odd)
+
+    for copy in sent + relays + [last]:
+        copy.wait_send()
+    for t in range(1, doms):
+        exchange(t).wait_send()
+    for d in range(doms):
+        @pl.when(me != d)
+        def _():
+            give(d).wait_send()
+    for j in range(bands):
+        @pl.when(z < j)
+        def _():
+            to_right(j).wait_send()
+
+        @pl.when(z > j)
+        def _():
+            to_left(j).wait_send()
+
+
+def fused(waves, cell_matrix, connect, send_index, rotation):
+    owned, width = waves.shape
+    slots = send_index.shape[2]
+    bands = lax.axis_size("band")
+    size = owned + 2 * slots
+    rows = owned // 2
+    doms = 8
+    vmem = pl.BlockSpec(memory_space=pltpu.VMEM)
+    f32, b16 = jnp.float32, jnp.bfloat16
+    dma = pltpu.SemaphoreType.DMA
+    return pl.pallas_call(
+        functools.partial(fused_kernel, bands, owned, slots),
+        out_shape=jax.ShapeDtypeStruct((owned, width), f32),
+        in_specs=[vmem] * 5,
+        out_specs=vmem,
+        scratch_shapes=[
+            pltpu.VMEM((bands, owned, width), f32),
+            pltpu.VMEM((bands, owned, width), f32),
+            pltpu.VMEM((bands, owned, width), f32),
+            pltpu.VMEM((doms, size + 8, size), f32),
+            pltpu.VMEM((doms, size, 2 * size), b16),
+            pltpu.VMEM((doms, 2 * slots, owned), b16),
+            pltpu.VMEM((doms, owned, 2 * slots), b16),
+            pltpu.VMEM((doms, rows, LANES), f32),
+            pltpu.VMEM((doms, rows, LANES), f32),
+            pltpu.VMEM((doms, 2 * size, LANES), b16),
+            pltpu.VMEM((doms, 2 * slots, LANES), b16),
+            pltpu.VMEM((doms, owned, LANES), f32),
+            pltpu.VMEM((doms, owned, LANES), f32),
+            pltpu.VMEM((doms, owned, LANES), f32),
+            pltpu.VMEM((doms, rows, LANES), f32),
+            pltpu.VMEM((doms, rows, LANES), f32),
+            dma((bands,)), dma((bands,)), dma((bands,)),
+            dma((7,)), dma((doms,)),
+            dma((doms,)), dma((doms,)),
+            dma((doms,)), dma((doms,)),
+        ],
+        compiler_params=pltpu.CompilerParams(
+            vmem_limit_bytes=56 * 2**20, collective_id=0, has_side_effects=True),
+        cost_estimate=pl.CostEstimate(
+            flops=DEGREE * doms * 4 * size * size * LANES, bytes_accessed=2**24, transcendentals=0),
+    )(waves, cell_matrix, connect, send_index, rotation)
+
+
 def shards(waves, cell_matrix, connect, send_index, rotation):
     owned = waves.shape[0]
     width = waves.shape[1]
     slots = send_index.shape[2]
     doms = lax.axis_size("dom")
+    if doms == 8 and width == doms * LANES // 2 and 2 * slots == LANES and lax.axis_size("band") == 4:
+        return fused(waves, cell_matrix, connect, send_index, rotation)
     size = owned + 2 * slots
     seat = jax.nn.one_hot(connect, size, dtype=jnp.float32)
     half_way = jnp.einsum("cij,cjn->cin", cell_matrix, seat, precision=lax.Precision.HIGH)

time: 129 us -> 92.5 us (0.72)
  the two profiles are of different devices: /device:TPU:0 before, /device:TPU:15 now
where the time goes in v1:
time: 92.5 us; the launch traced here: 92.3 us
  Pallas kernels  88.5 us (96%)
  local copies, waits for them, and re-layouts  3.8 us (4%)
    pallas_call x1, Pallas kernels, fused(): pl.pallas_call(functools.partial(fused_kernel, bands, owned, slots), out_...  88.5 us
    unnamed x2, local copies, waits for them, and re-layouts  3.8 us

profile of v1, /device:TPU:15, one launch (start us, length us, event | category | flops | bytes accessed | tf_op | source)
XLA Modules:
  0.0 92.3 jit_solution(4965414141767601778)
XLA Ops:
  0.0 1.9 %copy.6.cells = f32[8,125,125]{2,1,0:T(8,128)} copy(f32[8,125,125]{2,0,1:T(8,128)} %param.6) | data formatting | bytes 1000000 | tf_op args[1]
  1.9 88.5 %shard_map.55 = f32[256,512]{1,0:T(8,128)} custom-call(f32[256,512]{1,0:T(8,128)} %waves.1, f32[8,125,125]{2,1,0:T(8,128)} %copy.6.cells, s32[8,125]{1,0:T(8,128)} %conn.1, s32[1,2,64]{2,1,0:T(2,128)} %send.1, f32[512,2048]{1,0:T(8,128)} %rotation.1), custom_call_target="tpu_custom_call" | custom-call | flops 4831838208 | bytes 16777216 | tf_op jit(solution)/shard_map/pallas_call | solution.py:380
  90.4 1.9 %copy.8 = f32[256,512]{1,0:T(8,128)} copy(f32[256,512]{1,0:T(8,128)} %shard_map.55) | data formatting | bytes 1048576

commit v2 on v1

--- a/solution.py
+++ b/solution.py
@@ -132,15 +132,18 @@
     beside = lax.div(z + bands - 1, bands) + lax.div(2 * bands - 2 - z, bands)
     pl.semaphore_wait(barrier, doms - 1 + beside)
 
-    def to_right(j):
-        return pltpu.make_async_remote_copy(
-            src_ref=acc.at[j], dst_ref=from_left.at[j], send_sem=z_send.at[j],
-            recv_sem=z_right.at[j], device_id={"band": z + 1}, device_id_type=MESH)
-
-    def to_left(j):
-        return pltpu.make_async_remote_copy(
-            src_ref=acc.at[j], dst_ref=from_right.at[j], send_sem=z_send.at[j],
-            recv_sem=z_left.at[j], device_id={"band": z - 1}, device_id_type=MESH)
+    def part(h):
+        return pl.ds(h * rows, rows)
+
+    def to_right(j, h):
+        return pltpu.make_async_remote_copy(
+            src_ref=acc.at[j, part(h)], dst_ref=from_left.at[j, part(h)], send_sem=z_send.at[j, h],
+            recv_sem=z_right.at[j, h], device_id={"band": z + 1}, device_id_type=MESH)
+
+    def to_left(j, h):
+        return pltpu.make_async_remote_copy(
+            src_ref=acc.at[j, part(h)], dst_ref=from_right.at[j, part(h)], send_sem=z_send.at[j, h],
+            recv_sem=z_left.at[j, h], device_id={"band": z - 1}, device_id_type=MESH)
 
     order = []
     for r in range(bands // 2):
@@ -152,17 +155,19 @@
         if j > 0:
             @pl.when(z == 0)
             def _():
-                to_right(j).start()
+                for h in range(2):
+                    to_right(j, h).start()
         if j < bands - 1:
             @pl.when(z == bands - 1)
             def _():
-                to_left(j).start()
+                for h in range(2):
+                    to_left(j, h).start()
 
     node = lax.broadcasted_iota(jnp.int32, (size, conn.shape[1]), 0)
     total = jnp.zeros((size, size), jnp.float32)
-    for c in range(cells.shape[0]):
+    for c in range(cells.shape[1]):
         seat = jnp.where(node == conn[c : c + 1, :], 1.0, 0.0).astype(jnp.bfloat16)
-        a_high, a_low = high_low(cells[c])
+        a_high, a_low = high_low(cells[:, c, :])
         b_high, b_low = high_low(mm(seat, a_high) + mm(seat, a_low))
         dims = (((1,), (1,)), ((), ()))
         total = total + (
@@ -184,20 +189,23 @@
     for copy in sent:
         copy.start()
 
-    def relay_right(j, at):
+    def relay_right(j, at, h):
         @pl.when(z == at)
         def _():
-            to_right(j).wait_recv()
-            acc[j] = acc[j] + from_left[j]
-            to_right(j).start()
-
-    def relay_left(j, at):
+            to_right(j, h).wait_recv()
+            acc[j, part(h)] = acc[j, part(h)] + from_left[j, part(h)]
+            to_right(j, h).start()
+
+    def relay_left(j, at, h):
         @pl.when(z == at)
         def _():
-            to_left(j).wait_recv()
-            acc[j] = acc[j] + from_right[j]
-            to_left(j).start()
-
+            to_left(j, h).wait_recv()
+            acc[j, part(h)] = acc[j, part(h)] + from_right[j, part(h)]
+            to_left(j, h).start()
+
+    for h in range(2):
+        relay_right(3, 1, h)
+        relay_left(0, 2, h)
     pass_on(x_next, sib, 0).wait_recv()
     pass_on(y_next, sib, 0).wait_recv()
     relays = [
@@ -207,15 +215,14 @@
     ]
     for copy in relays:
         copy.start()
-    relay_right(3, 1)
-    relay_left(0, 2)
+    for h in range(2):
+        relay_left(0, 1, h)
+        relay_right(3, 2, h)
+        relay_right(2, 1, h)
+        relay_left(1, 2, h)
     pass_on(diag, sib, 6).wait_recv()
     last = pass_on(diag, sib, 6)
     last.start()
-    relay_left(0, 1)
-    relay_right(3, 2)
-    relay_right(2, 1)
-    relay_left(1, 2)
 
     lane = lax.broadcasted_iota(jnp.int32, (rows, LANES), 1)
     low_lanes = lane < half
@@ -239,42 +246,50 @@
     for d in range(doms):
         prepare(d)
 
+    quarter = rows // 2
+    low_quarter = lax.broadcasted_iota(jnp.int32, (quarter, LANES), 1) < half
+
+    def exchange(t, h):
+        to = lax.rem(me + t, doms)
+        share = pl.ds(h * quarter, quarter)
+        return pltpu.make_async_remote_copy(
+            src_ref=sendbuf.at[to, share], dst_ref=colrecv.at[me, share], send_sem=a_send.at[t, h],
+            recv_sem=a_recv.at[me, h], device_id={"dom": to}, device_id_type=MESH)
+
+    def arrival(t, h):
+        frm = lax.rem(me + t, doms)
+        share = pl.ds(h * quarter, quarter)
+        return pltpu.make_async_remote_copy(
+            src_ref=sendbuf.at[frm, share], dst_ref=colrecv.at[frm, share], send_sem=a_send.at[t, h],
+            recv_sem=a_recv.at[frm, h], device_id={"dom": frm}, device_id_type=MESH)
+
     finished = acc.at[z]
-    for j in range(bands):
-        if j > 0:
-            @pl.when(z == j)
-            def _():
-                to_right(j).wait_recv()
-                acc[j] = acc[j] + from_left[j]
-        if j < bands - 1:
-            @pl.when(z == j)
-            def _():
-                to_left(j).wait_recv()
-                acc[j] = acc[j] + from_right[j]
-
-    for p in range(doms // 2):
-        top = finished[:rows, p * LANES : (p + 1) * LANES]
-        bottom = finished[rows:, p * LANES : (p + 1) * LANES]
-        sendbuf[2 * p] = jnp.where(low_lanes, top, pltpu.roll(bottom, half, 1))
-        sendbuf[2 * p + 1] = jnp.where(low_lanes, pltpu.roll(top, half, 1), bottom)
-
-    def exchange(t):
-        to = lax.rem(me + t, doms)
-        return pltpu.make_async_remote_copy(
-            src_ref=sendbuf.at[to], dst_ref=colrecv.at[me], send_sem=a_send.at[t],
-            recv_sem=a_recv.at[me], device_id={"dom": to}, device_id_type=MESH)
-
-    def arrival(t):
-        frm = lax.rem(me + t, doms)
-        return pltpu.make_async_remote_copy(
-            src_ref=sendbuf.at[frm], dst_ref=colrecv.at[frm], send_sem=a_send.at[t],
-            recv_sem=a_recv.at[frm], device_id={"dom": frm}, device_id_type=MESH)
-
-    for t in range(1, doms):
-        exchange(t).start()
+    for h in range(2):
+        for j in range(bands):
+            if j > 0:
+                @pl.when(z == j)
+                def _():
+                    to_right(j, h).wait_recv()
+                    acc[j, part(h)] = acc[j, part(h)] + from_left[j, part(h)]
+            if j < bands - 1:
+                @pl.when(z == j)
+                def _():
+                    to_left(j, h).wait_recv()
+                    acc[j, part(h)] = acc[j, part(h)] + from_right[j, part(h)]
+        first, second = h * rows, h * rows + quarter
+        to_rows = slice(h * quarter, (h + 1) * quarter)
+        for p in range(doms // 2):
+            columns = slice(p * LANES, (p + 1) * LANES)
+            top = finished[first:second, columns]
+            bottom = finished[second : second + quarter, columns]
+            sendbuf[2 * p, to_rows] = jnp.where(low_quarter, top, pltpu.roll(bottom, half, 1))
+            sendbuf[2 * p + 1, to_rows] = jnp.where(low_quarter, pltpu.roll(top, half, 1), bottom)
+        for t in range(1, doms):
+            exchange(t, h).start()
     colrecv[me] = sendbuf[me]
-    for t in range(1, doms):
-        arrival(t).wait_recv()
+    for h in range(2):
+        for t in range(1, doms):
+            arrival(t, h).wait_recv()
 
     def put(d, v):
         x = packed(v, half)
@@ -284,8 +299,9 @@
     for d in range(doms):
         blk = colrecv[d]
         turned = pltpu.roll(blk, half, 1)
+        left, right = jnp.where(low_lanes, blk, turned), jnp.where(low_lanes, turned, blk)
         v = jnp.concatenate(
-            [jnp.where(low_lanes, blk, turned), jnp.where(low_lanes, turned, blk)], axis=0)
+            [left[:quarter], right[:quarter], left[quarter:], right[quarter:]], axis=0)
         state[d] = v
         before[d] = jnp.zeros_like(v)
         put(d, v)
@@ -352,19 +368,21 @@
     for copy in sent + relays + [last]:
         copy.wait_send()
     for t in range(1, doms):
-        exchange(t).wait_send()
+        for h in range(2):
+            exchange(t, h).wait_send()
     for d in range(doms):
         @pl.when(me != d)
         def _():
             give(d).wait_send()
     for j in range(bands):
-        @pl.when(z < j)
-        def _():
-            to_right(j).wait_send()
-
-        @pl.when(z > j)
-        def _():
-            to_left(j).wait_send()
+        for h in range(2):
+            @pl.when(z < j)
+            def _():
+                to_right(j, h).wait_send()
+
+            @pl.when(z > j)
+            def _():
+                to_left(j, h).wait_send()
 
 
 def fused(waves, cell_matrix, connect, send_index, rotation):
@@ -399,16 +417,16 @@
             pltpu.VMEM((doms, owned, LANES), f32),
             pltpu.VMEM((doms, rows, LANES), f32),
             pltpu.VMEM((doms, rows, LANES), f32),
-            dma((bands,)), dma((bands,)), dma((bands,)),
+            dma((bands, 2)), dma((bands, 2)), dma((bands, 2)),
             dma((7,)), dma((doms,)),
-            dma((doms,)), dma((doms,)),
+            dma((doms, 2)), dma((doms, 2)),
             dma((doms,)), dma((doms,)),
         ],
         compiler_params=pltpu.CompilerParams(
             vmem_limit_bytes=56 * 2**20, collective_id=0, has_side_effects=True),
         cost_estimate=pl.CostEstimate(
             flops=DEGREE * doms * 4 * size * size * LANES, bytes_accessed=2**24, transcendentals=0),
-    )(waves, cell_matrix, connect, send_index, rotation)
+    )(waves, jnp.swapaxes(cell_matrix, 0, 1), connect, send_index, rotation)
 
 
 def shards(waves, cell_matrix, connect, send_index, rotation):

time: 92.5 us -> 82.5 us (0.89)
  the two profiles are of different devices: /device:TPU:15 before, /device:TPU:23 now
where the time goes in v2:
time: 82.5 us; the launch traced here: 81.3 us
  Pallas kernels  79.4 us (96%)
  local copies, waits for them, and re-layouts  1.87 us (2%)
    pallas_call x1, Pallas kernels, fused(): pl.pallas_call(functools.partial(fused_kernel, bands, owned, slots), out_...  79.4 us
    unnamed x1, local copies, waits for them, and re-layouts  1.87 us

profile of v2, /device:TPU:23, one launch (start us, length us, event | category | flops | bytes accessed | tf_op | source)
XLA Modules:
  0.0 81.3 jit_solution(14119423806749038325)
XLA Ops:
  0.0 79.4 %shard_map.55 = f32[256,512]{1,0:T(8,128)} custom-call(f32[256,512]{1,0:T(8,128)} %waves.1, f32[125,8,125]{2,1,0:T(8,128)} %bitcast.1, s32[8,125]{1,0:T(8,128)} %conn.1, s32[1,2,64]{2,1,0:T(2,128)} %send.1, f32[512,2048]{1,0:T(8,128)} %rotation.1), custom_call_target="tpu_custom_call" | custom-call | flops 4831838208 | bytes 16777216 | tf_op jit(solution)/shard_map/pallas_call | solution.py:398
  79.5 1.9 %copy.7 = f32[256,512]{1,0:T(8,128)} copy(f32[256,512]{1,0:T(8,128)} %shard_map.55) | data formatting | bytes 1048576

commit v3 on v2

--- a/solution.py
+++ b/solution.py
@@ -10,6 +10,7 @@
 DEGREE = 8
 LANES = 128
 MESH = pl.DeviceIdType.MESH
+CUTS = 4
 
 
 centre = 5.5
@@ -132,8 +133,10 @@
     beside = lax.div(z + bands - 1, bands) + lax.div(2 * bands - 2 - z, bands)
     pl.semaphore_wait(barrier, doms - 1 + beside)
 
+    cut = owned // CUTS
+
     def part(h):
-        return pl.ds(h * rows, rows)
+        return pl.ds(h * cut, cut)
 
     def to_right(j, h):
         return pltpu.make_async_remote_copy(
@@ -155,12 +158,12 @@
         if j > 0:
             @pl.when(z == 0)
             def _():
-                for h in range(2):
+                for h in range(CUTS):
                     to_right(j, h).start()
         if j < bands - 1:
             @pl.when(z == bands - 1)
             def _():
-                for h in range(2):
+                for h in range(CUTS):
                     to_left(j, h).start()
 
     node = lax.broadcasted_iota(jnp.int32, (size, conn.shape[1]), 0)
@@ -203,7 +206,7 @@
             acc[j, part(h)] = acc[j, part(h)] + from_right[j, part(h)]
             to_left(j, h).start()
 
-    for h in range(2):
+    for h in range(CUTS):
         relay_right(3, 1, h)
         relay_left(0, 2, h)
     pass_on(x_next, sib, 0).wait_recv()
@@ -215,7 +218,7 @@
     ]
     for copy in relays:
         copy.start()
-    for h in range(2):
+    for h in range(CUTS):
         relay_left(0, 1, h)
         relay_right(3, 2, h)
         relay_right(2, 1, h)
@@ -246,7 +249,7 @@
     for d in range(doms):
         prepare(d)
 
-    quarter = rows // 2
+    quarter = cut // 2
     low_quarter = lax.broadcasted_iota(jnp.int32, (quarter, LANES), 1) < half
 
     def exchange(t, h):
@@ -264,7 +267,7 @@
             recv_sem=a_recv.at[frm, h], device_id={"dom": frm}, device_id_type=MESH)
 
     finished = acc.at[z]
-    for h in range(2):
+    for h in range(CUTS):
         for j in range(bands):
             if j > 0:
                 @pl.when(z == j)
@@ -276,7 +279,7 @@
                 def _():
                     to_left(j, h).wait_recv()
                     acc[j, part(h)] = acc[j, part(h)] + from_right[j, part(h)]
-        first, second = h * rows, h * rows + quarter
+        first, second = h * cut, h * cut + quarter
         to_rows = slice(h * quarter, (h + 1) * quarter)
         for p in range(doms // 2):
             columns = slice(p * LANES, (p + 1) * LANES)
@@ -287,7 +290,7 @@
         for t in range(1, doms):
             exchange(t, h).start()
     colrecv[me] = sendbuf[me]
-    for h in range(2):
+    for h in range(CUTS):
         for t in range(1, doms):
             arrival(t, h).wait_recv()
 
@@ -300,8 +303,11 @@
         blk = colrecv[d]
         turned = pltpu.roll(blk, half, 1)
         left, right = jnp.where(low_lanes, blk, turned), jnp.where(low_lanes, turned, blk)
-        v = jnp.concatenate(
-            [left[:quarter], right[:quarter], left[quarter:], right[quarter:]], axis=0)
+        sides = []
+        for h in range(CUTS):
+            at = slice(h * quarter, (h + 1) * quarter)
+            sides += [left[at], right[at]]
+        v = jnp.concatenate(sides, axis=0)
         state[d] = v
         before[d] = jnp.zeros_like(v)
         put(d, v)
@@ -368,14 +374,14 @@
     for copy in sent + relays + [last]:
         copy.wait_send()
     for t in range(1, doms):
-        for h in range(2):
+        for h in range(CUTS):
             exchange(t, h).wait_send()
     for d in range(doms):
         @pl.when(me != d)
         def _():
             give(d).wait_send()
     for j in range(bands):
-        for h in range(2):
+        for h in range(CUTS):
             @pl.when(z < j)
             def _():
                 to_right(j, h).wait_send()
@@ -417,9 +423,9 @@
             pltpu.VMEM((doms, owned, LANES), f32),
             pltpu.VMEM((doms, rows, LANES), f32),
             pltpu.VMEM((doms, rows, LANES), f32),
-            dma((bands, 2)), dma((bands, 2)), dma((bands, 2)),
+            dma((bands, CUTS)), dma((bands, CUTS)), dma((bands, CUTS)),
             dma((7,)), dma((doms,)),
-            dma((doms, 2)), dma((doms, 2)),
+            dma((doms, CUTS)), dma((doms, CUTS)),
             dma((doms,)), dma((doms,)),
         ],
         compiler_params=pltpu.CompilerParams(

time: 82.5 us -> 82 us (level); the launches traced: 81.3 us -> 81.9 us
  no operation moved by 1% of the time
where the time goes in v3:
time: 82 us; the launch traced here: 81.9 us
  Pallas kernels  80 us (98%)
  local copies, waits for them, and re-layouts  1.87 us (2%)
    pallas_call x1, Pallas kernels, fused(): pl.pallas_call(functools.partial(fused_kernel, bands, owned, slots), out_...  80 us
    unnamed x1, local copies, waits for them, and re-layouts  1.87 us

profile of v3, /device:TPU:23, one launch (start us, length us, event | category | flops | bytes accessed | tf_op | source)
XLA Modules:
  0.0 81.9 jit_solution(283733934874423351)
XLA Ops:
  0.0 80.0 %shard_map.55 = f32[256,512]{1,0:T(8,128)} custom-call(f32[256,512]{1,0:T(8,128)} %waves.1, f32[125,8,125]{2,1,0:T(8,128)} %bitcast.1, s32[8,125]{1,0:T(8,128)} %conn.1, s32[1,2,64]{2,1,0:T(2,128)} %send.1, f32[512,2048]{1,0:T(8,128)} %rotation.1), custom_call_target="tpu_custom_call" | custom-call | flops 4831838208 | bytes 16777216 | tf_op jit(solution)/shard_map/pallas_call | solution.py:404
  80.0 1.9 %copy.7 = f32[256,512]{1,0:T(8,128)} copy(f32[256,512]{1,0:T(8,128)} %shard_map.55) | data formatting | bytes 1048576

commit v4 on v3

--- a/solution.py
+++ b/solution.py
@@ -179,9 +179,12 @@
     r_at = lax.broadcasted_iota(jnp.int32, (size, size), 0)
     c_at = lax.broadcasted_iota(jnp.int32, (size, size), 1)
     shift = jnp.where((r_at == c_at) & (r_at < owned), centre, 0.0)
-    everyone[me, :size] = (total - shift) / half_width
-    everyone[me, size:] = jnp.zeros((8, size), jnp.float32)
-    everyone[me, size : size + 2, :slots] = send[0].astype(jnp.float32)
+    total = (total - shift) / half_width
+    everyone[me, :rows] = total[:rows]
+    everyone[me, rows:owned, rows:] = total[rows:owned, rows:]
+    everyone[me, rows:owned, :rows] = total[owned:, owned:]
+    everyone[me, owned:] = jnp.zeros((8, size), jnp.float32)
+    everyone[me, owned : owned + 2, :slots] = send[0].astype(jnp.float32)
 
     def pass_on(slot, to, k):
         return pltpu.make_async_remote_copy(
@@ -231,10 +234,18 @@
     low_lanes = lane < half
 
     def prepare(d):
-        m_high, m_low = high_low(everyone[d, :size])
+        upper_rows = everyone[d, :rows]
+        middle = everyone[d, rows:owned]
+        whole = jnp.concatenate([
+            upper_rows,
+            jnp.concatenate([jnp.transpose(upper_rows[:, rows:owned]), middle[:, rows:]], axis=1),
+            jnp.concatenate([
+                jnp.transpose(upper_rows[:, owned:]), jnp.transpose(middle[:, owned:]),
+                middle[:, :rows]], axis=1)], axis=0)
+        m_high, m_low = high_low(whole)
         matrix[d, :, :size] = m_high
         matrix[d, :, size:] = m_low
-        tile = everyone[d, size:, :LANES]
+        tile = everyone[d, owned:, :LANES]
         other = pltpu.roll(tile, half, 1)
         first_lanes = lax.broadcasted_iota(jnp.int32, (1, LANES), 1) < half
         row = jnp.where(first_lanes, tile[0:1], other[1:2]).astype(jnp.int32)
@@ -410,7 +421,7 @@
             pltpu.VMEM((bands, owned, width), f32),
             pltpu.VMEM((bands, owned, width), f32),
             pltpu.VMEM((bands, owned, width), f32),
-            pltpu.VMEM((doms, size + 8, size), f32),
+            pltpu.VMEM((doms, owned + 8, size), f32),
             pltpu.VMEM((doms, size, 2 * size), b16),
             pltpu.VMEM((doms, 2 * slots, owned), b16),
             pltpu.VMEM((doms, owned, 2 * slots), b16),
@@ -440,7 +451,7 @@
     width = waves.shape[1]
     slots = send_index.shape[2]
     doms = lax.axis_size("dom")
-    if doms == 8 and width == doms * LANES // 2 and 2 * slots == LANES and lax.axis_size("band") == 4:
+    if doms == 8 and width == doms * LANES // 2 and 2 * slots == LANES and owned == 2 * LANES and lax.axis_size("band") == 4:
         return fused(waves, cell_matrix, connect, send_index, rotation)
     size = owned + 2 * slots
     seat = jax.nn.one_hot(connect, size, dtype=jnp.float32)

time: 82 us -> 81.3 us (level)
  no operation moved by 1% of the time
where the time goes in v4:
time: 81.3 us; the launch traced here: 81.2 us
  Pallas kernels  79.3 us (98%)
  local copies, waits for them, and re-layouts  1.87 us (2%)
    pallas_call x1, Pallas kernels, fused(): pl.pallas_call(functools.partial(fused_kernel, bands, owned, slots), out_...  79.3 us
    unnamed x1, local copies, waits for them, and re-layouts  1.87 us

profile of v4, /device:TPU:23, one launch (start us, length us, event | category | flops | bytes accessed | tf_op | source)
XLA Modules:
  0.0 81.2 jit_solution(2616603891614991092)
XLA Ops:
  0.0 79.3 %shard_map.55 = f32[256,512]{1,0:T(8,128)} custom-call(f32[256,512]{1,0:T(8,128)} %waves.1, f32[125,8,125]{2,1,0:T(8,128)} %bitcast.1, s32[8,125]{1,0:T(8,128)} %conn.1, s32[1,2,64]{2,1,0:T(2,128)} %send.1, f32[512,2048]{1,0:T(8,128)} %rotation.1), custom_call_target="tpu_custom_call" | custom-call | flops 4831838208 | bytes 16777216 | tf_op jit(solution)/shard_map/pallas_call | solution.py:415
  79.3 1.9 %copy.7 = f32[256,512]{1,0:T(8,128)} copy(f32[256,512]{1,0:T(8,128)} %shard_map.55) | data formatting | bytes 1048576
